TPU v7x, 128 devices: a whole 4x4x4 slice. The times are simulated.
128 devices in a mesh: pair: 8 (over z_hi, y), blk: 16 (over z_lo, x, core).
Axes of the slice: x: 4, y: 4, z: 4 (z_hi: 2, z_lo: 2; z = z_hi * 2 + z_lo), core: 2. Of those that a mesh axis runs over, the one named last changes fastest.
Arguments:
- source: bfloat16 [32768, 1024], P(('pair', 'blk'))
- source_label: int32 [32768], P(('pair', 'blk')), may hold values from 0 to 7, as said below
- target: bfloat16 [32768, 1024], P(('pair', 'blk'))
- target_label: int32 [32768], P(('pair', 'blk')), may hold values from 0 to 7, as said below
Outputs:
- src_partner: float32 [32768, 1024], P(('pair', 'blk'))
- src_margin: float32 [32768], P(('pair', 'blk'))
- tgt_margin: float32 [32768], P(('pair', 'blk'))
Inputs may be any that keep to these rules, and one draw needn't show every extreme that they name: `source_label`: rows (i * 16 + k) * 256 to (i * 16 + k + 1) * 256 - 1 form block (i, k). For every k below 8, blocks (i, k) and (i, k + 8) together name every bucket exactly 64 times, so a block names one bucket at most 64 times, and in every draw some block names one bucket 64 times. `target_label`: rows (i * 16 + k) * 256 to (i * 16 + k + 1) * 256 - 1 form block (i, k). For every k below 8, blocks (i, k) and (i, k + 8) together name every bucket exactly 64 times, so a block names one bucket at most 64 times, and in every draw some block names one bucket 64 times.
All inputs are finite; a program needn't handle non-finite values.
Results may differ from a plain program's by a relative error of at most 0.0041.
Values may be sent and summed in bfloat16 or wider, within the bound.
No kernel may reach another device: no remote copies, remote signals or barrier semaphores. Data moves between devices by JAX's collectives and lax.ppermute only.
A program may use at most 128 MiB of HBM per device.

v0:
```python
import jax
import jax.numpy as jnp
from jax import lax
from jax.sharding import PartitionSpec as P

sharpness = 12.0


def normalize(row_block):
    values = row_block.astype(jnp.float32)
    square = jnp.mean(values * values, axis=-1, keepdims=True)
    return (values * lax.rsqrt(square + 1e-06)).astype(jnp.bfloat16)


def place_rows(labels, buckets, capacity):
    onehot = (labels[:, None] == jnp.arange(buckets, dtype=jnp.int32)[None, :]).astype(jnp.int32)
    before = jnp.cumsum(onehot, axis=0) - onehot
    slot_rank = jnp.sum(before * onehot, axis=1)
    return (labels * capacity + slot_rank, jnp.sum(onehot, axis=0))


def pack_rows(normed, slot_of, slot_total):
    return jnp.zeros((slot_total, normed.shape[1]), normed.dtype).at[slot_of].set(normed)


def safe_ratio(numer, denom):
    return numer / jnp.where(denom > 0.0, denom, 1.0)


def block_rows(length):
    best_size = 1
    for option in range(1, min(length, 512) + 1):
        if length % option == 0:
            best_size = option
    return best_size


def on_device(source, source_label, target, target_label):
    width = source.shape[1]
    own_rows = source.shape[0]
    buckets = lax.axis_size("pair")
    columns = lax.axis_size("blk")
    capacity = 2 * own_rows // buckets
    slot_total = buckets * capacity
    src_norm = normalize(source)
    tgt_norm = normalize(target)
    src_slot, src_count = place_rows(source_label, buckets, capacity)
    tgt_slot, tgt_count = place_rows(target_label, buckets, capacity)
    src_pack = pack_rows(src_norm, src_slot, slot_total).reshape(buckets, capacity, width)
    tgt_pack = pack_rows(tgt_norm, tgt_slot, slot_total).reshape(buckets, capacity, width)
    src_recv, tgt_recv, src_heard, tgt_heard = (
        lax.all_to_all(src_pack, "pair", split_axis=0, concat_axis=0, tiled=True),
        lax.all_to_all(tgt_pack, "pair", split_axis=0, concat_axis=0, tiled=True),
        lax.all_to_all(src_count, "pair", split_axis=0, concat_axis=0, tiled=True),
        lax.all_to_all(tgt_count, "pair", split_axis=0, concat_axis=0, tiled=True),
    )
    src_slots = src_recv.reshape(slot_total, width)
    tgt_slots = tgt_recv.reshape(slot_total, width)
    cap_spots = jnp.arange(capacity, dtype=jnp.int32)
    src_live = (cap_spots[None, :] < src_heard[:, None]).reshape(slot_total)
    tgt_live = (cap_spots[None, :] < tgt_heard[:, None]).reshape(slot_total)
    stay_live = src_live.astype(jnp.float32)
    move_live = tgt_live.astype(jnp.bfloat16)
    block_count = src_slots.shape[0]
    total_rows = columns * block_count

    def tile_weight(rows_block, live_block):
        similar = (
            lax.dot_general(
                src_slots, rows_block, (((1,), (1,)), ((), ())), preferred_element_type=jnp.float32
            )
            / width
        )
        weight = jnp.exp(sharpness * similar) * (
            stay_live[:, None] * live_block.astype(jnp.float32)[None, :]
        )
        return (similar, weight)

    zeros_rows = jnp.zeros((block_count,), jnp.float32)
    zeros_every = jnp.zeros((total_rows,), jnp.float32)
    held_init = jnp.zeros((1, 1), jnp.float32)
    first_init = (
        jnp.zeros((block_count, width), jnp.float32),
        zeros_rows,
        zeros_rows,
        zeros_every,
        zeros_every,
        held_init,
    )
    first_row = jnp.int32(0)
    part_rows = lax.all_gather(tgt_slots, "blk", axis=0, tiled=True)
    part_live = lax.all_gather(move_live, "blk", axis=0, tiled=True)
    length = part_rows.shape[0]
    step_rows = block_rows(length)

    def first_inner_step(block_index, state):
        partner_acc, fwd_total, fwd_sum, bwd_total, bwd_sum, held_tiles = state
        offset = block_index * step_rows
        rows_block = lax.dynamic_slice_in_dim(part_rows, offset, step_rows, 0)
        live_block = lax.dynamic_slice_in_dim(part_live, offset, step_rows, 0)
        similar, weight = tile_weight(rows_block, live_block)
        weighted = weight * similar
        partner_acc = partner_acc + jnp.dot(
            weight.astype(jnp.bfloat16), rows_block, preferred_element_type=jnp.float32
        )
        fwd_total = fwd_total + jnp.sum(weight, axis=1)
        fwd_sum = fwd_sum + jnp.sum(weighted, axis=1)
        bwd_total = lax.dynamic_update_slice_in_dim(
            bwd_total, jnp.sum(weight, axis=0), first_row + offset, 0
        )
        bwd_sum = lax.dynamic_update_slice_in_dim(
            bwd_sum, jnp.sum(weighted, axis=0), first_row + offset, 0
        )
        return (partner_acc, fwd_total, fwd_sum, bwd_total, bwd_sum, held_tiles)

    partner_acc, fwd_total, fwd_sum, part_total, part_sum, held_tiles = lax.fori_loop(
        0, length // step_rows, first_inner_step, first_init
    )
    summed_total, summed_weighted = lax.psum((part_total, part_sum), "blk")
    bwd_every = safe_ratio(summed_weighted, summed_total)
    own_index = lax.axis_index("blk")
    own_total = lax.dynamic_slice_in_dim(summed_total, own_index * block_count, block_count, 0)
    own_bwd = lax.dynamic_slice_in_dim(bwd_every, own_index * block_count, block_count, 0)
    fwd_stat = safe_ratio(fwd_sum, fwd_total)
    second_first_row = jnp.int32(0)
    second_part_rows = lax.all_gather(tgt_slots, "blk", axis=0, tiled=True)
    second_part_live = lax.all_gather(move_live, "blk", axis=0, tiled=True)
    length = second_part_rows.shape[0]
    second_step_rows = block_rows(length)

    def second_inner_step(block_index, state):
        back_acc, fore_part = state
        offset = block_index * second_step_rows
        rows_block = lax.dynamic_slice_in_dim(second_part_rows, offset, second_step_rows, 0)
        live_block = lax.dynamic_slice_in_dim(second_part_live, offset, second_step_rows, 0)
        similar, weight = tile_weight(rows_block, live_block)
        bwd_block = lax.dynamic_slice_in_dim(
            bwd_every, second_first_row + offset, second_step_rows, 0
        )
        back_acc = back_acc + jnp.dot(weight, bwd_block, precision=lax.Precision.HIGHEST)
        fore_block = jnp.dot(fwd_stat, weight, precision=lax.Precision.HIGHEST)
        fore_part = lax.dynamic_update_slice_in_dim(
            fore_part, fore_block, second_first_row + offset, 0
        )
        return (back_acc, fore_part)

    back_acc, fore_part = lax.fori_loop(
        0, length // second_step_rows, second_inner_step, (zeros_rows, zeros_every)
    )
    fore_own = lax.psum_scatter(
        fore_part.reshape(columns, block_count), "blk", scatter_dimension=0, tiled=True
    )[0]
    partner = safe_ratio(partner_acc, fwd_total[:, None])
    src_margin = fwd_stat - 0.5 * (fwd_stat + safe_ratio(back_acc, fwd_total))
    tgt_margin = own_bwd - 0.5 * (own_bwd + safe_ratio(fore_own, own_total))
    back_partner, back_src, back_tgt = (
        lax.all_to_all(
            partner.reshape(buckets, capacity, width),
            "pair",
            split_axis=0,
            concat_axis=0,
            tiled=True,
        ),
        lax.all_to_all(
            src_margin.reshape(buckets, capacity), "pair", split_axis=0, concat_axis=0, tiled=True
        ),
        lax.all_to_all(
            tgt_margin.reshape(buckets, capacity), "pair", split_axis=0, concat_axis=0, tiled=True
        ),
    )
    partner_out = back_partner.reshape(slot_total, width)[src_slot]
    src_out = back_src.reshape(slot_total)[src_slot]
    tgt_out = back_tgt.reshape(slot_total)[tgt_slot]
    return (partner_out, src_out, tgt_out)


def solution(mesh):
    return jax.shard_map(
        on_device,
        mesh=mesh,
        in_specs=(
            P(("pair", "blk"), None),
            P(("pair", "blk")),
            P(("pair", "blk"), None),
            P(("pair", "blk")),
        ),
        out_specs=(P(("pair", "blk"), None), P(("pair", "blk")), P(("pair", "blk"))),
        check_vma=False,
    )
```

profile of v0, /device:TPU:6, one launch (start us, length us, event | category | flops | bytes accessed | tf_op | source)
XLA Modules:
  0.0 529.9 jit_solution(6003493025504286049)
XLA Ops:
  14.1 24.9 %all_to_all.51 = bf16[8,64,1024]{2,1,0:T(8,128)(2,1)} all-to-all(bf16[8,64,1024]{2,1,0:T(8,128)(2,1)S(1)} %bitcast.88), channel_id=1, replica_groups=mesh['pair'=8,'blk'=16] {'pair'}, dimensions={0} | all-to-all | bytes 2097152 | tf_op jit(solution)/shard_map/all_to_all | solution.py:53
  39.6 3.3 all-to-all-start.3
  44.2 2.7 scatter_custom_fusion.1
  46.9 3.6 all-to-all-done.3
  50.5 11.0 %all_to_all.52 = s32[8,1,1]{2,1,0:T(1,128)S(1)} all-to-all(s32[8,1,1]{2,1,0:T(1,128)S(1)} %copy.10), channel_id=1, replica_groups=mesh['pair'=8,'blk'=16] {'pair'}, dimensions={0} | all-to-all | bytes 64 | tf_op jit(solution)/shard_map/all_to_all | solution.py:54
  61.5 4.2 all-to-all-start.1
  66.9 15.6 %all-gather = bf16[16,1,512]{2,1,0:T(2,128)(2,1)S(1)} all-gather(bf16[1,1,512]{2,1,0:T(2,128)(2,1)S(1)} %reshape.176), channel_id=1, replica_groups=mesh['pair'=8,'blk'=16] {'blk'}, dimensions={0}, use_global_device_ids=true | all-gather | bytes 17408 | tf_op jit(solution)/shard_map/all_gather | solution.py:92
  82.8 56.6 %all-gather.3.cloned.1.call-done = bf16[8192,1024]{1,0:T(8,128)(2,1)} async-done(((bf16[512,1024]{1,0:T(8,128)(2,1)}), bf16[8192,1024]{1,0:T(8,128)(2,1)}) %all-gather.3.cloned.1.call-update) | async-done | bytes 16777232 | tf_op jit(solution)/shard_map/all_gather | solution.py:91
  139.4 91.3 %while.42 = (s32[]{:T(128)}, f32[512,1024]{1,0:T(8,128)S(1)}, f32[512]{0:T(512)S(1)}, f32[512]{0:T(512)S(1)}, f32[8192]{0:T(1024)S(1)}, /*index=5*/f32[8192]{0:T...) while((s32[]{:T(128)}, f32[512,1024]{1,0:T(8,128)S(1)}, ...), condition=%wide.region_17.18_spmd.clone, body=%wide.region_12.17_spmd.clone.sunk | while | flops 1078199808 | bytes 9483506 | solution.py:116
  139.6 2.6 fusion.76
  145.3 2.6 fusion.76
  151.1 2.6 fusion.76
  156.8 2.6 fusion.76
  162.5 2.6 fusion.76
  168.2 2.6 fusion.76
  173.9 2.6 fusion.76
  179.7 2.6 fusion.76
  185.4 2.6 fusion.76
  191.1 2.6 fusion.76
  196.8 2.6 fusion.76
  202.5 2.6 fusion.76
  208.2 2.6 fusion.76
  214.0 2.6 fusion.76
  231.4 104.7 %all-reduce.4.cloned.1.call-done = (f32[8192]{0:T(1024)}, f32[8192]{0:T(1024)}) async-done(((f32[8192]{0:T(1024)}, f32[8192]{0:T(1024)}), (f32[8192]{0:T(1024)}, f32[8192]{0:T(1024)})) %all-reduce.4.cloned.1.call-update) | async-done | bytes 65552 | tf_op jit(solution)/shard_map/psum | solution.py:119
  336.9 71.7 %while.43 = (s32[]{:T(128)}, f32[512]{0:T(512)S(1)}, f32[8192]{0:T(1024)S(1)}, bf16[8192,1024]{1,0:T(8,128)(2,1)}, bf16[512,1024]{1,0:T(8,128)(2,1)}, /*index=5*...) while((s32[]{:T(128)}, f32[512]{0:T(512)S(1)}, ...), condition=%wide.region_21.22_spmd.clone, body=%wide.region_20.21_spmd.clone.sunk | while | flops 543951360 | bytes 5278949 | solution.py:147
  408.6 52.9 %all-reduce = f32[16,512]{1,0:T(8,128)S(1)} all-reduce(f32[16,512]{1,0:T(8,128)S(1)} %reshape.127), channel_id=2, replica_groups=mesh['pair'=8,'blk'=16] {'blk'}, use_global_device_ids=true, to_apply=%region_22.23.clone | all-reduce | flops 8192 | bytes 65536
  463.6 6.9 %all-to-all-start.6 = ((f32[8,1,64]{2,1,0:T(1,128)}), f32[8,1,64]{2,1,0:T(1,128)S(1)}, u32[]{:S(2)}, u32[]{:S(2)}) async-start(f32[8,1,64]{2,1,0:T(1,128)} %all_to_all.42), calls=%async_computation.6 | async-start | bytes 8192 | tf_op jit(solution)/shard_map/all_to_all | solution.py:167
  471.2 7.0 %all-to-all-done.6 = f32[8,1,64]{2,1,0:T(1,128)S(1)} async-done(((f32[8,1,64]{2,1,0:T(1,128)}), f32[8,1,64]{2,1,0:T(1,128)S(1)}, u32[]{:S(2)}, u32[]{:S(2)}) %all-to-all-start.6) | async-done | bytes 2080 | tf_op jit(solution)/shard_map/all_to_all | solution.py:167
  478.2 3.3 all-to-all-start.5
  483.1 5.9 %all-to-all-done.5 = f32[8,1,64]{2,1,0:T(1,128)S(1)} async-done(((f32[8,1,64]{2,1,0:T(1,128)}), f32[8,1,64]{2,1,0:T(1,128)S(1)}, u32[]{:S(2)}, u32[]{:S(2)}) %all-to-all-start.5) | async-done | bytes 2080 | tf_op jit(solution)/shard_map/all_to_all | solution.py:164
  489.0 3.6 all-to-all-start.4
  499.6 21.4 %all-to-all-done.4 = f32[8,64,1024]{2,1,0:T(8,128)S(1)} async-done(((f32[8,64,1024]{2,1,0:T(8,128)}), f32[8,64,1024]{2,1,0:T(8,128)S(1)}, u32[]{:S(2)}, u32[]{:S(2)}) %all-to-all-start.4) | async-done | bytes 2097184 | tf_op jit(solution)/shard_map/all_to_all | solution.py:157
  (327 shorter events, 150.3 us)
Async XLA Ops:
  7.2 132.2 %all-gather.3.cloned.1.call-start = ((), (), s32[]{:S(2)}) async-start(), calls=%async_computation.7 | async-start | bytes 17825792 | tf_op jit(solution)/shard_map/all_gather | solution.py:91
  11.5 31.4 %copy-start.3 = (s32[256]{0:T(256)S(1)}, s32[256]{0:T(256)}, u32[]{:S(2)}) copy-start(s32[256]{0:T(256)} %param.9) | copy-start | bytes 3076
  11.5 32.5 %copy-start = (bf16[256,1024]{1,0:T(8,128)(2,1)S(1)}, bf16[256,1024]{1,0:T(8,128)(2,1)}, u32[]{:S(2)}) copy-start(bf16[256,1024]{1,0:T(8,128)(2,1)} %param.8) | copy-start | bytes 1572868
  39.6 10.8 %all-to-all-start.3 = ((s32[8,1,1]{2,1,0:T(1,128)}), s32[8,1,1]{2,1,0:T(1,128)S(1)}, u32[]{:S(2)}, u32[]{:S(2)}) async-start(s32[8,1,1]{2,1,0:T(1,128)} %copy.9), calls=%async_computation.3 | async-start | bytes 8192 | tf_op jit(solution)/shard_map/all_to_all | solution.py:55
  44.0 21.8 %copy-start.4 = (u32[128]{0:T(128)S(1)}, u32[128]{0:T(128)}, u32[]{:S(2)}) copy-start(u32[128]{0:T(128)} %constant.168) | copy-start | bytes 1540
  61.5 21.3 %all-to-all-start.1 = ((bf16[8,64,1024]{2,1,0:T(8,128)(2,1)}), bf16[8,64,1024]{2,1,0:T(8,128)(2,1)}, u32[]{:S(2)}, u32[]{:S(2)}) async-start(bf16[8,64,1024]{2,1,0:T(8,128)(2,1)} %bitcast.8), calls=%async_computation.1 | async-start | bytes 2097152 | tf_op jit(solution)/shard_map/all_to_all | solution.py:52
  65.7 270.3 %all-reduce.4.cloned.1.call-start = ((), (), s32[]{:S(2)}) async-start(), calls=%async_computation.8 | async-start | bytes 131072 | tf_op jit(solution)/shard_map/psum | solution.py:119
  230.7 0.6 copy-start.1
  230.7 0.6 copy-start.2
  463.6 14.5 %all-to-all-start.6 = ((f32[8,1,64]{2,1,0:T(1,128)}), f32[8,1,64]{2,1,0:T(1,128)S(1)}, u32[]{:S(2)}, u32[]{:S(2)}) async-start(f32[8,1,64]{2,1,0:T(1,128)} %all_to_all.42), calls=%async_computation.6 | async-start | bytes 8192 | tf_op jit(solution)/shard_map/all_to_all | solution.py:167
  478.2 10.8 %all-to-all-start.5 = ((f32[8,1,64]{2,1,0:T(1,128)}), f32[8,1,64]{2,1,0:T(1,128)S(1)}, u32[]{:S(2)}, u32[]{:S(2)}) async-start(f32[8,1,64]{2,1,0:T(1,128)} %all_to_all.40), calls=%async_computation.5 | async-start | bytes 8192 | tf_op jit(solution)/shard_map/all_to_all | solution.py:164
  489.0 32.1 %all-to-all-start.4 = ((f32[8,64,1024]{2,1,0:T(8,128)}), f32[8,64,1024]{2,1,0:T(8,128)S(1)}, u32[]{:S(2)}, u32[]{:S(2)}) async-start(f32[8,64,1024]{2,1,0:T(8,128)} %bitcast.86), calls=%async_computation.4 | async-start | bytes 4194304 | tf_op jit(solution)/shard_map/all_to_all | solution.py:157
Sparse Core Ops, SparseCore 0:
  39.1 100.2 all-gather.2
  231.5 104.5 all-reduce.3
where the time goes:
time: 532 us; the launch traced here: 530 us
  waiting for transfers between devices  199 us (37%)
  matrix products  142 us (27%)
  blocking collectives  104 us (20%)
  local copies, waits for them, and re-layouts  27.3 us (5%)
  starting transfers between devices  21.4 us (4%)
  other arithmetic  20.6 us (4%)
  between operations  14.3 us (3%)
    psum x1, waiting for transfers between devices, on_device(): summed_total, summed_weighted = lax.psum((part_total, part_sum), 'blk')  105 us
    dot_general x32, matrix products, tile_weight(): lax.dot_general(src_slots, rows_block, (((1,), (1,)), ((), ())), preferre...  79 us
    all_gather x1, waiting for transfers between devices, on_device(): part_rows = lax.all_gather(tgt_slots, 'blk', axis=0, tiled=True)  56.6 us
    unnamed x1, blocking collectives  52.9 us
    dot_general x16, matrix products, first_inner_step(): jnp.dot(weight.astype(jnp.bfloat16), rows_block, preferred_element_type=j...  36.7 us
    all_to_all x1, blocking collectives, on_device(): lax.all_to_all(tgt_pack, 'pair', split_axis=0, concat_axis=0, tiled=True)  24.9 us
    all_to_all x1, waiting for transfers between devices, on_device(): lax.all_to_all(partner.reshape(buckets, capacity, width), 'pair', split_a...  21.4 us
    dot_general x16, matrix products, second_inner_step(): fore_block = jnp.dot(fwd_stat, weight, precision=lax.Precision.HIGHEST)  15.7 us
  transfers between devices with their start and end apart: 7, of which 6 were waited for; matrix products, arithmetic and copies ran while one was open for 3% of the time, Pallas kernels for 0%

commit v1 on v0

--- a/solution.py
+++ b/solution.py
@@ -88,7 +88,10 @@
         held_init,
     )
     first_row = jnp.int32(0)
-    part_rows = lax.all_gather(tgt_slots, "blk", axis=0, tiled=True)
+    devices = lax.axis_size("blk")
+    parts = jnp.stack([tgt_slots for _ in range(devices)])
+    parts = lax.all_to_all(parts, "blk", split_axis=0, concat_axis=0)
+    part_rows = jnp.concatenate(parts, axis=0)
     part_live = lax.all_gather(move_live, "blk", axis=0, tiled=True)
     length = part_rows.shape[0]
     step_rows = block_rows(length)

time: 532 us -> 810 us (1.52)
  blocking collectives: 104 us -> 318 us
  waiting for transfers between devices: 199 us -> 246 us
  starting transfers between devices: 21.4 us -> 30.3 us
    all_gather x1, blocking collectives: 15.6 us -> 233 us  [on_device(): part_live = lax.all_gather(move_live, 'blk', axis=0, tiled=True)]
    all_gather x1, waiting for transfers between devices: 56.6 us -> 96.6 us  [on_device(): second_part_rows = lax.all_gather(tgt_slots, 'blk', axis=0, tiled=True)]
    all_to_all x1 -> x2, waiting for transfers between devices: 0.01 us -> 13.2 us  [the longest x1 13.2 us: on_device(): lax.all_to_all(tgt_pack, 'pair', split_axis=0, concat_axis=0, tiled=True)]
  transfers between devices with their start and end apart: 7 -> 8, of which waited for: 6 -> 6; matrix products, arithmetic and copies ran while one was open for 3% -> 3% of each run, Pallas kernels for 0% -> 0%
where the time goes in v1:
time: 810 us; the launch traced here: 808 us
  blocking collectives  318 us (39%)
  waiting for transfers between devices  246 us (30%)
  matrix products  143 us (18%)
  local copies, waits for them, and re-layouts  33.3 us (4%)
  starting transfers between devices  30.3 us (4%)
  other arithmetic  22 us (3%)
  between operations  14.3 us (2%)
    all_gather x1, blocking collectives, on_device(): part_live = lax.all_gather(move_live, 'blk', axis=0, tiled=True)  233 us
    psum x1, waiting for transfers between devices, on_device(): summed_total, summed_weighted = lax.psum((part_total, part_sum), 'blk')  101 us
    all_gather x1, waiting for transfers between devices, on_device(): second_part_rows = lax.all_gather(tgt_slots, 'blk', axis=0, tiled=True)  96.6 us
    dot_general x32, matrix products, tile_weight(): lax.dot_general(src_slots, rows_block, (((1,), (1,)), ((), ())), preferre...  79.2 us
    unnamed x1, blocking collectives  50.3 us
    dot_general x16, matrix products, first_inner_step(): jnp.dot(weight.astype(jnp.bfloat16), rows_block, preferred_element_type=j...  37.2 us
    all_to_all x1, waiting for transfers between devices, on_device(): lax.all_to_all(partner.reshape(buckets, capacity, width), 'pair', split_a...  21.4 us
    all_to_all x1, blocking collectives, on_device(): lax.all_to_all(src_pack, 'pair', split_axis=0, concat_axis=0, tiled=True)  20.4 us
  transfers between devices with their start and end apart: 8, of which 6 were waited for; matrix products, arithmetic and copies ran while one was open for 3% of the time, Pallas kernels for 0%

profile of v1, /device:TPU:6, one launch (start us, length us, event | category | flops | bytes accessed | tf_op | source)
XLA Modules:
  0.0 807.7 jit_solution(14959612080226981171)
XLA Ops:
  10.2 7.8 all-to-all-start.4
  22.5 3.2 scatter_custom_fusion
  25.7 14.7 %all_to_all.56 = s32[8,1,1]{2,1,0:T(1,128)S(1)} all-to-all(s32[8,1,1]{2,1,0:T(1,128)S(1)} %copy.10), channel_id=1, replica_groups=mesh['pair'=8,'blk'=16] {'pair'}, dimensions={0} | all-to-all | bytes 64 | tf_op jit(solution)/shard_map/all_to_all | solution.py:54
  40.3 3.6 all-to-all-start
  46.1 13.2 %all-to-all-done = bf16[8,64,1024]{2,1,0:T(8,128)(2,1)S(1)} async-done(((bf16[8,64,1024]{2,1,0:T(8,128)(2,1)}), bf16[8,64,1024]{2,1,0:T(8,128)(2,1)S(1)}, u32[]{:S(2)}, u32[]{:S(2)}) %all-to-all-start) | async-done | bytes 1048608 | tf_op jit(solution)/shard_map/all_to_all | solution.py:53
  59.3 20.4 %all_to_all.57 = bf16[8,64,1024]{2,1,0:T(8,128)(2,1)} all-to-all(bf16[8,64,1024]{2,1,0:T(8,128)(2,1)S(1)} %bitcast.90), channel_id=1, replica_groups=mesh['pair'=8,'blk'=16] {'pair'}, dimensions={0} | all-to-all | bytes 2097152 | tf_op jit(solution)/shard_map/all_to_all | solution.py:52
  79.8 5.9 stack.3
  85.7 5.4 all-to-all-start.1
  91.6 232.9 %all-gather = bf16[16,1,512]{2,1,0:T(2,128)(2,1)S(1)} all-gather(bf16[1,1,512]{2,1,0:T(2,128)(2,1)S(1)} %reshape.179), channel_id=1, replica_groups=mesh['pair'=8,'blk'=16] {'blk'}, dimensions={0}, use_global_device_ids=true | all-gather | bytes 17408 | tf_op jit(solution)/shard_map/all_gather | solution.py:95
  324.8 92.0 %while.42 = (s32[]{:T(128)}, f32[512,1024]{1,0:T(8,128)S(1)}, f32[512]{0:T(512)S(1)}, f32[512]{0:T(512)S(1)}, f32[8192]{0:T(1024)S(1)}, /*index=5*/f32[8192]{0:T...) while((s32[]{:T(128)}, f32[512,1024]{1,0:T(8,128)S(1)}, ...), condition=%wide.region_17.18_spmd.clone, body=%wide.region_12.17_spmd.clone.sunk | while | flops 1078199808 | bytes 9483506 | solution.py:119
  325.1 2.6 fusion.76
  330.8 2.6 fusion.76
  336.6 2.6 fusion.76
  342.4 2.6 fusion.76
  348.1 2.6 fusion.76
  353.9 2.6 fusion.76
  359.6 2.6 fusion.76
  365.4 2.6 fusion.76
  371.2 2.6 fusion.76
  376.9 2.6 fusion.76
  382.7 2.6 fusion.76
  388.4 2.6 fusion.76
  418.9 101.3 %all-reduce.4.cloned.1.call-done = (f32[8192]{0:T(1024)}, f32[8192]{0:T(1024)}) async-done(((f32[8192]{0:T(1024)}, f32[8192]{0:T(1024)}), (f32[8192]{0:T(1024)}, f32[8192]{0:T(1024)})) %all-reduce.4.cloned.1.call-update) | async-done | bytes 65552 | tf_op jit(solution)/shard_map/psum | solution.py:122
  520.9 96.6 %all-gather.3.cloned.1.call-done = bf16[8192,1024]{1,0:T(8,128)(2,1)} async-done(((bf16[512,1024]{1,0:T(8,128)(2,1)}), bf16[8192,1024]{1,0:T(8,128)(2,1)}) %all-gather.3.cloned.1.call-update) | async-done | bytes 16777232 | tf_op jit(solution)/shard_map/all_gather | solution.py:129
  617.5 71.7 %while.43 = (s32[]{:T(128)}, f32[512]{0:T(512)S(1)}, f32[8192]{0:T(1024)S(1)}, bf16[8192,1024]{1,0:T(8,128)(2,1)}, bf16[512,1024]{1,0:T(8,128)(2,1)}, /*index=5*...) while((s32[]{:T(128)}, f32[512]{0:T(512)S(1)}, ...), condition=%wide.region_21.22_spmd.clone, body=%wide.region_20.21_spmd.clone.sunk | while | flops 543951360 | bytes 5278949 | solution.py:150
  689.3 50.3 %all-reduce = f32[16,512]{1,0:T(8,128)S(1)} all-reduce(f32[16,512]{1,0:T(8,128)S(1)} %reshape.130), channel_id=2, replica_groups=mesh['pair'=8,'blk'=16] {'blk'}, use_global_device_ids=true, to_apply=%region_22.23.clone | all-reduce | flops 8192 | bytes 65536
  741.7 6.6 all-to-all-start.7
  749.0 7.0 all-to-all-done.7
  755.9 3.3 all-to-all-start.6
  760.8 5.9 all-to-all-done.6
  766.8 3.6 all-to-all-start.5
  777.4 21.4 %all-to-all-done.5 = f32[8,64,1024]{2,1,0:T(8,128)S(1)} async-done(((f32[8,64,1024]{2,1,0:T(8,128)}), f32[8,64,1024]{2,1,0:T(8,128)S(1)}, u32[]{:S(2)}, u32[]{:S(2)}) %all-to-all-start.5) | async-done | bytes 2097184 | tf_op jit(solution)/shard_map/all_to_all | solution.py:160
  (332 shorter events, 157.8 us)
Async XLA Ops:
  10.2 15.5 %all-to-all-start.4 = ((s32[8,1,1]{2,1,0:T(1,128)}), s32[8,1,1]{2,1,0:T(1,128)S(1)}, u32[]{:S(2)}, u32[]{:S(2)}) async-start(s32[8,1,1]{2,1,0:T(1,128)} %copy.9), calls=%async_computation.4 | async-start | bytes 8192 | tf_op jit(solution)/shard_map/all_to_all | solution.py:55
  18.7 25.2 %copy-start.1 = (bf16[256,1024]{1,0:T(8,128)(2,1)S(1)}, bf16[256,1024]{1,0:T(8,128)(2,1)}, u32[]{:S(2)}) copy-start(bf16[256,1024]{1,0:T(8,128)(2,1)} %param.8) | copy-start | bytes 1572868
  22.5 21.6 %copy-start.4 = (s32[256]{0:T(256)S(1)}, s32[256]{0:T(256)}, u32[]{:S(2)}) copy-start(s32[256]{0:T(256)} %param.9) | copy-start | bytes 3076
  40.3 19.0 %all-to-all-start = ((bf16[8,64,1024]{2,1,0:T(8,128)(2,1)}), bf16[8,64,1024]{2,1,0:T(8,128)(2,1)S(1)}, u32[]{:S(2)}, u32[]{:S(2)}) async-start(bf16[8,64,1024]{2,1,0:T(8,128)(2,1)} %bitcast.3), calls=%async_computation | async-start | bytes 2097152 | tf_op jit(solution)/shard_map/all_to_all | solution.py:53
  59.3 26.4 %copy-start = (bf16[8,64,1024]{2,1,0:T(8,128)(2,1)}, bf16[8,64,1024]{2,1,0:T(8,128)(2,1)S(1)}, u32[]{:S(2)}) copy-start(bf16[8,64,1024]{2,1,0:T(8,128)(2,1)S(1)} %all-to-all-done) | copy-start | bytes 3145732
  85.7 239.1 %all-to-all-start.1 = ((bf16[16,512,1024]{2,1,0:T(8,128)(2,1)}), bf16[16,512,1024]{2,1,0:T(8,128)(2,1)}, u32[]{:S(2)}, u32[]{:S(2)}) async-start(bf16[16,512,1024]{2,1,0:T(8,128)(2,1)} %stack.3), calls=%async_computation.1 | async-start | bytes 33554432 | tf_op jit(solution)/shard_map/all_to_all | solution.py:93
  91.1 429.0 %all-reduce.4.cloned.1.call-start = ((), (), s32[]{:S(2)}) async-start(), calls=%async_computation.9 | async-start | bytes 131072 | tf_op jit(solution)/shard_map/psum | solution.py:122
  324.8 93.5 %copy-start.5 = (u32[128]{0:T(128)S(1)}, u32[128]{0:T(128)}, u32[]{:S(2)}) copy-start(u32[128]{0:T(128)} %constant.168) | copy-start | bytes 1540
  416.9 0.6 copy-start.2
  416.9 0.6 copy-start.3
  417.5 200.0 %all-gather.3.cloned.1.call-start = ((), (), s32[]{:S(2)}) async-start(), calls=%async_computation.8 | async-start | bytes 17825792 | tf_op jit(solution)/shard_map/all_gather | solution.py:129
  741.7 14.3 %all-to-all-start.7 = ((f32[8,1,64]{2,1,0:T(1,128)}), f32[8,1,64]{2,1,0:T(1,128)S(1)}, u32[]{:S(2)}, u32[]{:S(2)}) async-start(f32[8,1,64]{2,1,0:T(1,128)} %all_to_all.46), calls=%async_computation.7 | async-start | bytes 8192 | tf_op jit(solution)/shard_map/all_to_all | solution.py:170
  755.9 10.8 %all-to-all-start.6 = ((f32[8,1,64]{2,1,0:T(1,128)}), f32[8,1,64]{2,1,0:T(1,128)S(1)}, u32[]{:S(2)}, u32[]{:S(2)}) async-start(f32[8,1,64]{2,1,0:T(1,128)} %all_to_all.44), calls=%async_computation.6 | async-start | bytes 8192 | tf_op jit(solution)/shard_map/all_to_all | solution.py:167
  766.8 32.1 %all-to-all-start.5 = ((f32[8,64,1024]{2,1,0:T(8,128)}), f32[8,64,1024]{2,1,0:T(8,128)S(1)}, u32[]{:S(2)}, u32[]{:S(2)}) async-start(f32[8,64,1024]{2,1,0:T(8,128)} %bitcast.89), calls=%async_computation.5 | async-start | bytes 4194304 | tf_op jit(solution)/shard_map/all_to_all | solution.py:160
Sparse Core Ops, SparseCore 0:
  417.6 102.4 all-reduce.3
  522.5 94.9 all-gather.2
